TPU v7x, 512 devices: a whole 4x4x16 slice. The times are simulated.
512 devices in a mesh: dp: 64 (over z_lo, y, core), tensor: 8 (over z_hi, x).
Axes of the slice: x: 4, y: 4, z: 16 (z_hi: 2, z_lo: 8; z = z_hi * 8 + z_lo), core: 2. Of those that a mesh axis runs over, the one named last changes fastest.
Arguments:
- tokens: bfloat16 [16384, 1024], P('dp'), may hold values from -6 to 6
- hidden_grad: bfloat16 [16384, 14336], P('dp', 'tensor'), may hold values from -6 to 6
- gate: bfloat16 [16384, 14336], P('dp', 'tensor'), may hold values from -8 to 8
- up: bfloat16 [16384, 14336], P('dp', 'tensor'), may hold values from -6 to 6
- gate_weight: bfloat16 [1024, 14336], P('dp', 'tensor'), may hold values from -0.046875 to 0.046875
- up_weight: bfloat16 [1024, 14336], P('dp', 'tensor'), may hold values from -0.046875 to 0.046875
Outputs:
- input_grad: bfloat16 [16384, 1024], P('dp', 'tensor')
- act_cov: float32 [1024, 1024], P('tensor')
- grad_cov: float32 [1024, 1024], P('tensor')
All inputs are finite; a program needn't handle non-finite values.
Results may differ from a plain program's by a relative error of at most 0.0049.
Values may be sent and summed in bfloat16 or wider, within the bound.
A program may use at most 64 MiB of HBM per device.

v0:
```python
import jax
import jax.numpy as jnp
from jax import lax
from jax.sharding import PartitionSpec as P


def project(left, piece):
    return lax.dot_general(
        left, piece, (((1,), (1,)), ((), ())), preferred_element_type=jnp.float32
    )


def gram_rows(matrix, start, share):
    own_cols = lax.dynamic_slice_in_dim(matrix, start, share, 1)
    return lax.dot_general(
        own_cols, matrix, (((0,), (0,)), ((), ())), preferred_element_type=jnp.float32
    )


def shards(tokens, hidden_grad, gate, up, gate_weight, up_weight):
    grad32 = hidden_grad.astype(jnp.float32)
    gate32 = gate.astype(jnp.float32)
    up32 = up.astype(jnp.float32)
    sig = jax.nn.sigmoid(gate32)
    grad_gate = (grad32 * up32 * sig * (1.0 + gate32 * (1.0 - sig))).astype(jnp.bfloat16)
    grad_up = (grad32 * gate32 * sig).astype(jnp.bfloat16)
    features = tokens.shape[1]
    partial_sum = project(grad_gate, lax.all_gather(gate_weight, "dp", axis=0, tiled=True))
    partial_sum = partial_sum + project(
        grad_up, lax.all_gather(up_weight, "dp", axis=0, tiled=True)
    )
    share = features // lax.axis_size("tensor")
    offset = lax.axis_index("tensor") * share
    summed = lax.psum(partial_sum, "tensor")
    full_grad = summed.astype(jnp.bfloat16)
    own_grad = lax.dynamic_slice_in_dim(full_grad, offset, share, 1)
    count = tokens.shape[0] * lax.axis_size("dp")
    act_rows = gram_rows(tokens, offset, share) / count
    grad_rows = gram_rows(full_grad, offset, share) / count
    act_cov, grad_cov = lax.psum((act_rows, grad_rows), "dp")
    return (own_grad, act_cov, grad_cov)


def solution(mesh):
    placed = (
        P("dp", None),
        P("dp", "tensor"),
        P("dp", "tensor"),
        P("dp", "tensor"),
        P("dp", "tensor"),
        P("dp", "tensor"),
    )
    return jax.shard_map(
        shards,
        mesh=mesh,
        in_specs=placed,
        out_specs=(P("dp", "tensor"), P("tensor", None), P("tensor", None)),
        check_vma=False,
    )
```

profile of v0, /device:TPU:1, one launch (start us, length us, event | category | flops | bytes accessed | tf_op | source)
XLA Modules:
  0.0 1287.6 jit_solution(13298347500530493567)
XLA Ops:
  7.2 0.0 copy-start
  7.2 0.0 all-gather.3.cloned.1.call-start
  7.2 0.7 all-gather.3.cloned.1.call-update
  7.9 0.0 all-gather.5.cloned.1.call-start
  8.0 0.7 all-gather.5.cloned.1.call-update
  8.7 0.0 all-reduce.4.cloned.1.call-start
  8.7 0.0 copy-done
  8.7 1.1 convolution_multiply_fusion.1
  9.8 0.0 copy-start.2
  9.8 0.0 copy-start.3
  9.8 128.8 %all-gather.3.cloned.1.call-done = bf16[1024,1792]{1,0:T(8,128)(2,1)} async-done(((bf16[16,1792]{1,0:T(8,128)(2,1)}), bf16[1024,1792]{1,0:T(8,128)(2,1)}) %all-gather.3.cloned.1.call-update) | async-done | bytes 3670032 | tf_op jit(solution)/shard_map/all_gather | solution.py:28
  138.6 5.4 fusion.11
  144.0 115.1 %all-gather.5.cloned.1.call-done = bf16[1024,1792]{1,0:T(8,128)(2,1)} async-done(((bf16[16,1792]{1,0:T(8,128)(2,1)}), bf16[1024,1792]{1,0:T(8,128)(2,1)}) %all-gather.5.cloned.1.call-update) | async-done | bytes 3670032 | tf_op jit(solution)/shard_map/all_gather | solution.py:30
  259.1 0.0 copy-done.2
  259.1 0.0 copy-done.3
  259.1 3.5 convolution_add_fusion
  262.6 150.9 %all-reduce.5 = bf16[256,1024]{1,0:T(8,128)(2,1)S(1)} all-reduce(f32[256,1024]{1,0:T(8,128)S(1)} %convolution_add_fusion), channel_id=1, replica_groups=mesh['dp'=64,'tensor'=8] {'tensor'}, use_global_device_ids=true, to_apply=%region_0.0 | all-reduce | flops 262144 | bytes 1572864 | tf_op jit(solution)/shard_map/psum | solution.py:34
  413.6 0.0 copy-start.1
  413.6 1.0 convolution_multiply_fusion
  414.6 0.0 all-reduce.4.cloned.1.call-update
  414.7 862.7 %all-reduce.4.cloned.1.call-done = (f32[128,1024]{1,0:T(8,128)}, f32[128,1024]{1,0:T(8,128)}) async-done(((f32[128,1024]{1,0:T(8,128)}, f32[128,1024]{1,0:T(8,128)}), (f32[128,1024]{1,0:T(8,128)}, f32[128,1024]{1,0:T(8,128)})) %all-reduce.4.cloned.1.call-update) | async-done | bytes 1048592 | tf_op jit(solution)/shard_map/psum | solution.py:40
  1277.3 1.9 copy.13
  1279.2 1.9 copy.14
  1281.1 0.0 copy-done.1
  (1 shorter events, 0.0 us)
Async XLA Ops:
  7.2 1.6 copy-start
  7.2 131.4 %all-gather.3.cloned.1.call-start = ((), (), s32[]{:S(2)}) async-start(), calls=%async_computation | async-start | bytes 3727360 | tf_op jit(solution)/shard_map/all_gather | solution.py:28
  7.9 251.1 %all-gather.5.cloned.1.call-start = ((), (), s32[]{:S(2)}) async-start(), calls=%async_computation.1 | async-start | bytes 3727360 | tf_op jit(solution)/shard_map/all_gather | solution.py:30
  8.7 1268.7 %all-reduce.4.cloned.1.call-start = ((), (), s32[]{:S(2)}) async-start(), calls=%async_computation.2 | async-start | bytes 2097152 | tf_op jit(solution)/shard_map/psum | solution.py:40
  9.8 249.3 %copy-start.2 = (bf16[256,1792]{1,0:T(8,128)(2,1)S(1)}, bf16[256,1792]{1,0:T(8,128)(2,1)}, u32[]{:S(2)}) copy-start(bf16[256,1792]{1,0:T(8,128)(2,1)} %param.7) | copy-start | bytes 2752516
  9.8 249.3 %copy-start.3 = (bf16[256,1792]{1,0:T(8,128)(2,1)S(1)}, bf16[256,1792]{1,0:T(8,128)(2,1)}, u32[]{:S(2)}) copy-start(bf16[256,1792]{1,0:T(8,128)(2,1)} %param.8) | copy-start | bytes 2752516
  413.6 867.5 %copy-start.1 = (bf16[256,128]{1,0:T(8,128)(2,1)}, bf16[256,128]{1,0:T(8,128)(2,1)S(1)}, u32[]{:S(2)}) copy-start(bf16[256,128]{1,0:T(8,128)(2,1)S(1)} %constant_dynamic-slice_fusion) | copy-start | bytes 196612
Sparse Core Ops, SparseCore 0:
  10.2 128.3 all-gather.2
  140.7 118.2 all-gather.4
  414.8 862.5 all-reduce.3
where the time goes:
time: 1290 us
  waiting for transfers between devices  1110 us (86%)
  blocking collectives  151 us (12%)
  between operations  13.8 us (1%)
    psum x1, waiting for transfers between devices, shards(): act_cov, grad_cov = lax.psum((act_rows, grad_rows), 'dp')  863 us
    psum x1, blocking collectives, shards(): summed = lax.psum(partial_sum, 'tensor')  151 us
    all_gather x1, waiting for transfers between devices, shards(): lax.all_gather(gate_weight, 'dp', axis=0, tiled=True)  129 us
    all_gather x1, waiting for transfers between devices, shards(): lax.all_gather(up_weight, 'dp', axis=0, tiled=True)  115 us
  transfers between devices with their start and end apart: 3, of which 3 were waited for; matrix products, arithmetic and copies ran while one was open for 1% of the time, Pallas kernels for 0%

commit v1 on v0

v1 whole, which is shorter than its diff:
```python
import jax
import jax.numpy as jnp
from jax import lax
from jax.experimental import pallas as pl
from jax.experimental.pallas import tpu as pltpu
from jax.sharding import PartitionSpec as P

BF16 = jnp.bfloat16
F32 = jnp.float32
NT = (((1,), (1,)), ((), ()))
TN = (((0,), (0,)), ((), ()))
COUNT = 16384


def kernel(
    tok_hbm, hid_hbm, gate_hbm, up_hbm, gw_hbm, uw_hbm,
    ig_out, act_out, cov_out,
    tok, vin, acts, w, pown, xs, xr, zsb, zrb, gbuf, swp, gfull,
    covp, d0r, d1s, d1r, d2s, d2r, fin,
    loc_sem, as_s, as_r, zs_s, z_r, ys_s, y_r, y2s_s, y2_r,
    xs_s, xs_r, z8_s, z8_r, sw_s, sw_r, xg_s, xg_r,
    d0_s, d0_r, d1_s, d1_r, d2_s, d2_r, d3_s, d3_r, d4_s, d4_r, d5_s, d5_r,
):
    i = lax.axis_index("dp")
    j = lax.axis_index("tensor")
    c = lax.rem(i, 2)
    y = lax.rem(lax.div(i, 2), 4)
    z = lax.div(i, 8)
    x = lax.rem(j, 4)
    zh = lax.div(j, 4)
    oc = 1 - c

    def dev(z_=z, y_=y, c_=c, zh_=zh, x_=x):
        return ((z_ * 4 + y_) * 2 + c_, zh_ * 4 + x_)

    def remote(src, dst, ss, rs, to):
        return pltpu.make_async_remote_copy(
            src_ref=src, dst_ref=dst, send_sem=ss, recv_sem=rs,
            device_id=to, device_id_type=pl.DeviceIdType.MESH,
        )

    sib = dev(c_=oc)

    def ymod(k):
        return lax.rem(y + k, 4)

    def xmod(k):
        return lax.rem(x + k, 4)

    def zmod(k):
        return lax.rem(z + k, 8)

    def chunk(zz, yy):
        return w.at[lax.rem(zz, 4), :, lax.div(zz, 4), yy]

    def half(zz, yy, g):
        return w.at[lax.rem(zz, 4), g, lax.div(zz, 4), yy]

    loads = [
        pltpu.make_async_copy(gw_hbm, half(z, y, 0), loc_sem.at[0]),
        pltpu.make_async_copy(uw_hbm, half(z, y, 1), loc_sem.at[1]),
        pltpu.make_async_copy(hid_hbm, vin.at[0], loc_sem.at[2]),
        pltpu.make_async_copy(gate_hbm, vin.at[1], loc_sem.at[3]),
        pltpu.make_async_copy(up_hbm, vin.at[2], loc_sem.at[4]),
        pltpu.make_async_copy(tok_hbm, tok, loc_sem.at[5]),
    ]
    for load in loads:
        load.start()

    barrier = pltpu.get_barrier_semaphore()
    partners = [sib]
    partners += [dev(y_=ymod(k)) for k in range(1, 4)]
    partners += [dev(x_=xmod(k)) for k in range(1, 4)]
    partners += [dev(z_=zmod(k)) for k in range(1, 8)]
    partners += [dev(zh_=1 - zh)]
    for to in partners:
        pl.semaphore_signal(
            barrier, inc=1, device_id=to, device_id_type=pl.DeviceIdType.MESH
        )
    for load in loads:
        load.wait()

    def act_rows(r, _):
        rows = pl.ds(pl.multiple_of(r * 16, 16), 16)
        h32 = vin[0, rows, :].astype(F32)
        g32 = vin[1, rows, :].astype(F32)
        u32 = vin[2, rows, :].astype(F32)
        sig = jax.nn.sigmoid(g32)
        hs = h32 * sig
        acts[c, 0, rows, :] = (hs * u32 * (1.0 + g32 * (1.0 - sig))).astype(BF16)
        acts[c, 1, rows, :] = (hs * g32).astype(BF16)
        return 0

    lax.fori_loop(0, 16, act_rows, 0)

    own_tok = tok[:, pl.ds(pl.multiple_of(j * 128, 128), 128)]
    for k in range(8):
        covp[0, k] = lax.dot_general(
            own_tok, tok[:, k * 128:(k + 1) * 128], TN, preferred_element_type=F32
        )

    pl.semaphore_wait(barrier, 15)

    def z_up(zz):
        return remote(chunk(zz, y), chunk(zz, y), zs_s.at[0, zz], z_r.at[zz], dev(z_=z + 1))

    def z_dn(zz):
        return remote(chunk(zz, y), chunk(zz, y), zs_s.at[1, zz], z_r.at[zz], dev(z_=z - 1))

    def y_send(zz, d):
        to = dev(y_=ymod(1 if d == 0 else 3))
        return remote(chunk(zz, y), chunk(zz, y), ys_s.at[d, zz], y_r.at[d, zz], to)

    def y_recv(zz, d):
        src = ymod(3 if d == 0 else 1)
        return remote(chunk(zz, src), chunk(zz, src), ys_s.at[d, zz], y_r.at[d, zz], sib)

    def y2_send(zz, d):
        src = ymod(3 if d == 0 else 1)
        to = dev(y_=ymod(1 if d == 0 else 3))
        return remote(half(zz, src, d), half(zz, src, d), y2s_s.at[d, zz], y2_r.at[d, zz], to)

    def y2_recv(zz, d):
        src = ymod(2)
        return remote(half(zz, src, d), half(zz, src, d), y2s_s.at[d, zz], y2_r.at[d, zz], sib)

    def each(s, fn):
        @pl.when((s >= 0) & (z - s >= 0) & (z - s <= 7))
        def _():
            fn(z - s, 0)

        @pl.when((s >= 1) & (z + s <= 7))
        def _():
            fn(z + s, 1)

    def arrive_z(s):
        def fn(zz, d):
            @pl.when(s > 0)
            def _():
                remote(chunk(zz, y), chunk(zz, y), zs_s.at[0, zz], z_r.at[zz], sib).wait_recv()

            if d == 0:
                @pl.when(z < 7)
                def _():
                    z_up(zz).start()

                @pl.when((s == 0) & (z > 0))
                def _():
                    z_dn(zz).start()
            else:
                @pl.when(z > 0)
                def _():
                    z_dn(zz).start()
            y_send(zz, 0).start()
            y_send(zz, 1).start()
        return fn

    def arrive_y(zz, _):
        for d in range(2):
            y_recv(zz, d).wait_recv()
            y2_send(zz, d).start()

    def arrive_y2(zz, _):
        for d in range(2):
            y2_recv(zz, d).wait_recv()

    def ready(t):
        below = jnp.abs(z - t)
        above = jnp.abs(z - t - 4)
        return jnp.maximum(below, above)

    def x_send(t):
        return remote(xs.at[t], xr.at[x], xs_s.at[t], xs_r.at[x], dev(x_=t))

    def block(t, s):
        @pl.when(ready(t) == s)
        def _():
            wg = w[t, 0].reshape(128, 1792)
            wu = w[t, 1].reshape(128, 1792)
            for cc in range(2):
                part = lax.dot_general(acts[cc, 0], wg, NT, preferred_element_type=F32)
                part += lax.dot_general(acts[cc, 1], wu, NT, preferred_element_type=F32)

                @pl.when(t == x)
                def _():
                    pown[cc] = part

                @pl.when(t != x)
                def _():
                    xs[t, cc] = part.astype(BF16)

            @pl.when(t != x)
            def _():
                x_send(t).start()
        return s

    z8 = remote(zsb, zrb, z8_s, z8_r, dev(zh_=1 - zh))
    act_copy = remote(acts.at[c], acts.at[c], as_s, as_r, sib)
    act_back = remote(acts.at[oc], acts.at[oc], as_s, as_r, sib)

    def x_sum():
        for k in range(1, 4):
            src = xmod(k)
            remote(xs.at[0], xr.at[src], xs_s.at[src], xs_r.at[src], sib).wait_recv()
        for cc in range(2):
            total = pown[cc]
            for k in range(1, 4):
                total = total + xr[xmod(k), cc].astype(F32)
            pown[cc] = total
            zsb[cc] = total.astype(BF16)
        z8.start()

    def step(s, _):
        each(s, arrive_z(s))

        @pl.when(s == 0)
        def _():
            act_copy.start()
            d0_send(0).start()

        each(s - 1, arrive_y)

        @pl.when(s == 2)
        def _():
            act_back.wait_recv()

        each(s - 2, arrive_y2)
        lax.fori_loop(0, 4, block, s - 2)

        @pl.when(ready(x) == s - 3)
        def _():
            x_sum()
        return 0

    def d0_send(m):
        rows = pl.ds(pl.multiple_of(oc * 64, 64), 64)
        return remote(covp.at[m, :, rows], d0r.at[m], d0_s.at[m], d0_r.at[m], sib)

    def d1_send(m, k):
        to = ymod(k)
        return remote(d1s.at[m, to], d1r.at[m, y], d1_s.at[m, to], d1_r.at[m, y], dev(y_=to))

    def d1_recv(m, k):
        src = ymod(k)
        return remote(d1s.at[m, src], d1r.at[m, src], d1_s.at[m, src], d1_r.at[m, src], sib)

    def d2_send(m, k):
        to = zmod(k)
        return remote(d2s.at[m, to], d2r.at[m, z], d2_s.at[m, to], d2_r.at[m, z], dev(z_=to))

    def d2_recv(m, k):
        src = zmod(k)
        return remote(d2s.at[m, src], d2r.at[m, src], d2_s.at[m, src], d2_r.at[m, src], sib)

    def d3_send(m, k):
        to = zmod(k)
        piece = fin.at[m, c, y, z]
        return remote(piece, piece, d3_s.at[m, to], d3_r.at[m, z], dev(z_=to))

    def d3_recv(m, k):
        src = zmod(k)
        piece = fin.at[m, c, y, src]
        return remote(piece, piece, d3_s.at[m, src], d3_r.at[m, src], sib)

    def d4_send(m, k):
        to = ymod(k)
        piece = fin.at[m, c, y]
        return remote(piece, piece, d4_s.at[m, to], d4_r.at[m, y], dev(y_=to))

    def d4_recv(m, k):
        src = ymod(k)
        piece = fin.at[m, c, src]
        return remote(piece, piece, d4_s.at[m, src], d4_r.at[m, src], sib)

    def d5_send(m):
        return remote(fin.at[m, c], fin.at[m, c], d5_s.at[m], d5_r.at[m], sib)

    def d5_recv(m):
        return remote(fin.at[m, oc], fin.at[m, oc], d5_s.at[m], d5_r.at[m], sib)

    def core_sum(m):
        d0_send(m).wait_recv()
        for yy in range(4):
            rows = pl.ds(pl.multiple_of(c * 64 + yy * 16, 16), 16)
            total = covp[m, :, rows, :] + d0r[m, :, yy * 16:(yy + 1) * 16, :]
            covp[m, :, rows, :] = total
            d1s[m, yy] = total.astype(BF16)
        for k in (2, 1, 3):
            d1_send(m, k).start()

    def y_sum(m):
        rows = pl.ds(pl.multiple_of(c * 64 + y * 16, 16), 16)
        total = covp[m, :, rows, :]
        for k in (1, 3, 2):
            d1_recv(m, k).wait_recv()
            total = total + d1r[m, ymod(k)].astype(F32)
        covp[m, :, rows, :] = total
        d2s[m] = total.astype(BF16)
        for k in range(1, 8):
            d2_send(m, k).start()

    def z_sum(m):
        rows = pl.ds(pl.multiple_of(c * 64 + y * 16, 16), 16)
        total = covp[m, z, rows, :]
        for k in range(1, 8):
            d2_recv(m, k).wait_recv()
            total = total + d2r[m, zmod(k)].astype(F32)
        fin[m, c, y, z] = (total * (1.0 / COUNT)).astype(BF16)
        for k in range(1, 8):
            d3_send(m, k).start()

    def z_back(m):
        for k in range(1, 8):
            d3_recv(m, k).wait_recv()
        for k in (2, 1, 3):
            d4_send(m, k).start()

    def y_back(m):
        for k in (1, 3, 2):
            d4_recv(m, k).wait_recv()
        d5_send(m).start()

    def write(m, out, cc):
        for yy in range(4):
            rows = pl.ds(pl.multiple_of(cc * 64 + yy * 16, 16), 16)
            for k in range(8):
                out[rows, k * 128:(k + 1) * 128] = fin[m, cc, yy, k].astype(F32)

    lax.fori_loop(0, 11, step, 0)

    core_sum(0)
    y_sum(0)

    z8.wait_recv()
    for cc in range(2):
        gbuf[cc] = (pown[cc] + zrb[cc].astype(F32)).astype(BF16)
    swap = remote(gbuf.at[oc], swp, sw_s, sw_r, sib)
    swap.start()

    src_i = lax.broadcasted_iota(jnp.int32, (256, 256), 0)
    dst_i = lax.broadcasted_iota(jnp.int32, (256, 256), 1)
    d_half, d_y = lax.div(dst_i, 128), lax.rem(lax.div(dst_i, 32), 4)
    d_core, d_row = lax.rem(lax.div(dst_i, 16), 2), lax.rem(dst_i, 16)
    own_first = lax.rem(d_core + c, 2)
    perm = (src_i == own_first * 128 + d_half * 64 + d_y * 16 + d_row).astype(F32).astype(BF16)

    swap.wait_recv()
    own_half = gbuf[c]
    both = lax.dot_general(
        own_half, perm[:128], (((1,), (0,)), ((), ())), preferred_element_type=F32
    ) + lax.dot_general(
        swp[...], perm[128:], (((1,), (0,)), ((), ())), preferred_element_type=F32
    )
    gfull[x] = both.astype(BF16)

    def xg_send(k):
        to = xmod(k)
        return remote(gfull.at[x], gfull.at[x], xg_s.at[to], xg_r.at[x], dev(x_=to))

    def xg_recv(k):
        src = xmod(k)
        return remote(gfull.at[src], gfull.at[src], xg_s.at[src], xg_r.at[src], sib)

    for k in (2, 1, 3):
        xg_send(k).start()
    own = gfull[x, :, pl.ds(pl.multiple_of(zh * 128, 128), 128)]
    ig_out[...] = own

    def cov_cols(k):
        xx = xmod(k)
        part = lax.dot_general(own, gfull[xx], TN, preferred_element_type=F32)
        covp[1, xx] = part[:, :128]
        covp[1, xx + 4] = part[:, 128:]

    cov_cols(0)
    z_sum(0)
    for k in (1, 3, 2):
        xg_recv(k).wait_recv()
        cov_cols(k)
    d0_send(1).start()
    core_sum(1)
    z_back(0)
    y_sum(1)
    y_back(0)
    write(0, act_out, c)
    d5_recv(0).wait_recv()
    write(0, act_out, oc)
    z_sum(1)
    z_back(1)
    y_back(1)
    write(1, cov_out, c)
    d5_recv(1).wait_recv()
    write(1, cov_out, oc)

    act_copy.wait_send()
    z8.wait_send()
    swap.wait_send()

    def drain(zz, _):
        @pl.when((z < 7) & (zz <= z))
        def _():
            z_up(zz).wait_send()

        @pl.when((z > 0) & (zz >= z))
        def _():
            z_dn(zz).wait_send()

        for d in range(2):
            y_send(zz, d).wait_send()
            y2_send(zz, d).wait_send()
        return 0

    lax.fori_loop(0, 8, drain, 0)
    for k in range(1, 4):
        x_send(xmod(k)).wait_send()
        xg_send(k).wait_send()
    for m in range(2):
        d0_send(m).wait_send()
        for k in range(1, 4):
            d1_send(m, k).wait_send()
            d4_send(m, k).wait_send()
        for k in range(1, 8):
            d2_send(m, k).wait_send()
            d3_send(m, k).wait_send()
        d5_send(m).wait_send()


def shards(tokens, hidden_grad, gate, up, gate_weight, up_weight):
    sem = pltpu.SemaphoreType.DMA
    return pl.pallas_call(
        kernel,
        out_shape=(
            jax.ShapeDtypeStruct((256, 128), BF16),
            jax.ShapeDtypeStruct((128, 1024), F32),
            jax.ShapeDtypeStruct((128, 1024), F32),
        ),
        in_specs=[pl.BlockSpec(memory_space=pl.ANY)] * 6,
        out_specs=tuple([pl.BlockSpec(memory_space=pltpu.VMEM)] * 3),
        scratch_shapes=[
            pltpu.VMEM((256, 1024), BF16),
            pltpu.VMEM((3, 256, 1792), BF16),
            pltpu.VMEM((2, 2, 256, 1792), BF16),
            pltpu.VMEM((4, 2, 2, 4, 16, 1792), BF16),
            pltpu.VMEM((2, 256, 128), F32),
            pltpu.VMEM((4, 2, 256, 128), BF16),
            pltpu.VMEM((4, 2, 256, 128), BF16),
            pltpu.VMEM((2, 256, 128), BF16),
            pltpu.VMEM((2, 256, 128), BF16),
            pltpu.VMEM((2, 256, 128), BF16),
            pltpu.VMEM((256, 128), BF16),
            pltpu.VMEM((4, 256, 256), BF16),
            pltpu.VMEM((2, 8, 128, 128), F32),
            pltpu.VMEM((2, 8, 64, 128), F32),
            pltpu.VMEM((2, 4, 8, 16, 128), BF16),
            pltpu.VMEM((2, 4, 8, 16, 128), BF16),
            pltpu.VMEM((2, 8, 16, 128), BF16),
            pltpu.VMEM((2, 8, 16, 128), BF16),
            pltpu.VMEM((2, 2, 4, 8, 16, 128), BF16),
            sem((6,)), sem, sem,
            sem((2, 8)), sem((8,)),
            sem((2, 8)), sem((2, 8)),
            sem((2, 8)), sem((2, 8)),
            sem((4,)), sem((4,)),
            sem, sem, sem, sem,
            sem((4,)), sem((4,)),
            sem((2,)), sem((2,)),
            sem((2, 4)), sem((2, 4)),
            sem((2, 8)), sem((2, 8)),
            sem((2, 8)), sem((2, 8)),
            sem((2, 4)), sem((2, 4)),
            sem((2,)), sem((2,)),
        ],
        compiler_params=pltpu.CompilerParams(
            collective_id=1, has_side_effects=True, vmem_limit_bytes=44 << 20
        ),
        cost_estimate=pl.CostEstimate(
            flops=2_500_000_000, bytes_accessed=10_000_000, transcendentals=1_000_000
        ),
        name="kfac_stats",
    )(tokens, hidden_grad, gate, up, gate_weight, up_weight)


def solution(mesh):
    placed = (
        P("dp", None),
        P("dp", "tensor"),
        P("dp", "tensor"),
        P("dp", "tensor"),
        P("dp", "tensor"),
        P("dp", "tensor"),
    )
    return jax.shard_map(
        shards,
        mesh=mesh,
        in_specs=placed,
        out_specs=(P("dp", "tensor"), P("tensor", None), P("tensor", None)),
        check_vma=False,
    )
```

time: 1290 us -> 117 us (0.09)
  waiting for transfers between devices: 1110 us -> 0 us
  blocking collectives: 151 us -> 0 us
  Pallas kernels: 0 us -> 108 us
  between operations: 13.8 us -> 0.65 us
    psum x1 -> x0, waiting for transfers between devices: 863 us -> none  [shards(): act_cov, grad_cov = lax.psum((act_rows, grad_rows), 'dp')]
    all_gather x2 -> x0, waiting for transfers between devices: 244 us -> none  [the longest x1 129 us: shards(): lax.all_gather(gate_weight, 'dp', axis=0, tiled=True)]
    psum x1 -> x0, blocking collectives: 151 us -> none  [shards(): summed = lax.psum(partial_sum, 'tensor')]
    pallas_call x0 -> x1, Pallas kernels: none -> 108 us  [shards(): pl.pallas_call(kernel, out_shape=(jax.ShapeDtypeStruct((256, 128), BF16),...]
  transfers between devices with their start and end apart: 3 -> 0, of which waited for: 3 -> 0; matrix products, arithmetic and copies ran while one was open for 1% -> 0% of each run, Pallas kernels for 0% -> 0%
where the time goes in v1:
time: 117 us
  Pallas kernels  108 us (92%)
  local copies, waits for them, and re-layouts  8.42 us (7%)
    pallas_call x1, Pallas kernels, shards(): pl.pallas_call(kernel, out_shape=(jax.ShapeDtypeStruct((256, 128), BF16),...  108 us
    unnamed x15, local copies, waits for them, and re-layouts  8.42 us

profile of v1, /device:TPU:1, one launch (start us, length us, event | category | flops | bytes accessed | tf_op | source)
XLA Modules:
  0.0 116.9 jit_solution(9940379674129812937)
XLA Ops:
  0.6 0.0 copy-start
  0.6 1.2 %copy-done = bf16[256,1792]{1,0:T(8,128)(2,1)S(1)} copy-done((bf16[256,1792]{1,0:T(8,128)(2,1)S(1)}, bf16[256,1792]{1,0:T(8,128)(2,1)}, u32[]{:S(2)}) %copy-start) | copy-done | bytes 917528
  1.8 0.0 copy-start.1
  1.8 1.2 %copy-done.1 = bf16[256,1792]{1,0:T(8,128)(2,1)S(1)} copy-done((bf16[256,1792]{1,0:T(8,128)(2,1)S(1)}, bf16[256,1792]{1,0:T(8,128)(2,1)}, u32[]{:S(2)}) %copy-start.1) | copy-done | bytes 917528
  3.0 0.0 copy-start.2
  3.0 1.2 %copy-done.2 = bf16[256,1792]{1,0:T(8,128)(2,1)S(1)} copy-done((bf16[256,1792]{1,0:T(8,128)(2,1)S(1)}, bf16[256,1792]{1,0:T(8,128)(2,1)}, u32[]{:S(2)}) %copy-start.2) | copy-done | bytes 917528
  4.2 0.0 copy-start.3
  4.2 1.0 copy-done.3
  5.2 0.0 copy-start.4
  5.2 0.8 copy-done.4
  6.0 0.0 copy-start.5
  6.0 0.8 copy-done.5
  6.9 107.8 %kfac_stats.1 = (bf16[256,128]{1,0:T(8,128)(2,1)S(1)}, f32[128,1024]{1,0:T(8,128)S(1)}, f32[128,1024]{1,0:T(8,128)S(1)}) custom-call(bf16[256,1024]{1,0:T(8,128)(2,1)S(1)} %copy-done.3, bf16[256,1792]{1,0:T(8,128)(2,1)S(1)} %copy-done, bf16[256,1792]{1,0:T(8,128)(2,1)S(1)} %copy-done.1, bf16[256,1792]{1,0:T(8,128)(2,1)S(1)} %copy-done.2, ...), custom_call_target="tpu_custom_call" | custom-call | flops 2500000000 | bytes 10000000 | tf_op jit(solution)/shard_map/kfac_stats/pallas_call | solution.py:430
  114.6 0.6 copy.12
  115.3 0.8 copy.13
  116.1 0.8 copy.14
Async XLA Ops:
  0.6 1.2 %copy-start = (bf16[256,1792]{1,0:T(8,128)(2,1)S(1)}, bf16[256,1792]{1,0:T(8,128)(2,1)}, u32[]{:S(2)}) copy-start(bf16[256,1792]{1,0:T(8,128)(2,1)} %hid_hbm.1) | copy-start | bytes 2752516
  1.8 1.2 %copy-start.1 = (bf16[256,1792]{1,0:T(8,128)(2,1)S(1)}, bf16[256,1792]{1,0:T(8,128)(2,1)}, u32[]{:S(2)}) copy-start(bf16[256,1792]{1,0:T(8,128)(2,1)} %gate_hbm.1) | copy-start | bytes 2752516
  3.0 1.2 %copy-start.2 = (bf16[256,1792]{1,0:T(8,128)(2,1)S(1)}, bf16[256,1792]{1,0:T(8,128)(2,1)}, u32[]{:S(2)}) copy-start(bf16[256,1792]{1,0:T(8,128)(2,1)} %up_hbm.1) | copy-start | bytes 2752516
  4.2 1.0 copy-start.3
  5.2 0.8 copy-start.4
  6.0 0.8 copy-start.5

commit v2 on v1

v2 whole, which is shorter than its diff:
```python
import jax
import jax.numpy as jnp
from jax import lax
from jax.experimental import pallas as pl
from jax.experimental.pallas import tpu as pltpu
from jax.sharding import PartitionSpec as P

BF16 = jnp.bfloat16
F32 = jnp.float32
NT = (((1,), (1,)), ((), ()))
TN = (((0,), (0,)), ((), ()))
COUNT = 16384
LAG = 3
STOP = 9


def kernel(
    tok_hbm, hid_hbm, gate_hbm, up_hbm, gw_hbm, uw_hbm,
    fin_out, own_out,
    tok, vin, acts, w, pown, xs, xr, zsb, zrb, gs, gt,
    covp, d0r, d1s, d1r, d2s, d2r, fin,
    loc_sem, as_s, as_r, zs_s, z_r, ys_s, y_r, y2s_s, y2_r,
    xs_s, xs_r, z8_s, z8_r, xg_s, xg_r, out_sem,
    d0_s, d0_r, d1_s, d1_r, d2_s, d2_r, d3_s, d3_r, d4_s, d4_r, d5_s, d5_r, hello_sem,
):
    i = lax.axis_index("dp")
    j = lax.axis_index("tensor")
    c = lax.rem(i, 2)
    y = lax.rem(lax.div(i, 2), 4)
    z = lax.div(i, 8)
    x = lax.rem(j, 4)
    zh = lax.div(j, 4)
    oc = 1 - c

    def dev(z_=z, y_=y, c_=c, zh_=zh, x_=x):
        return ((z_ * 4 + y_) * 2 + c_, zh_ * 4 + x_)

    def remote(src, dst, ss, rs, to):
        return pltpu.make_async_remote_copy(
            src_ref=src, dst_ref=dst, send_sem=ss, recv_sem=rs,
            device_id=to, device_id_type=pl.DeviceIdType.MESH,
        )

    sib = dev(c_=oc)

    def ymod(k):
        return lax.rem(y + k, 4)

    def xmod(k):
        return lax.rem(x + k, 4)

    def zmod(k):
        return lax.rem(z + k, 8)

    def chunk(zz, yy):
        return w.at[lax.rem(zz, 4), :, lax.div(zz, 4), yy]

    def half(zz, yy, g):
        return w.at[lax.rem(zz, 4), g, lax.div(zz, 4), yy]

    loads = [
        pltpu.make_async_copy(gw_hbm, half(z, y, 0), loc_sem.at[0]),
        pltpu.make_async_copy(uw_hbm, half(z, y, 1), loc_sem.at[1]),
        pltpu.make_async_copy(hid_hbm, vin.at[0], loc_sem.at[2]),
        pltpu.make_async_copy(gate_hbm, vin.at[1], loc_sem.at[3]),
        pltpu.make_async_copy(up_hbm, vin.at[2], loc_sem.at[4]),
        pltpu.make_async_copy(tok_hbm, tok, loc_sem.at[5]),
    ]
    for load in loads:
        load.start()

    barrier = pltpu.get_barrier_semaphore()
    zf = zh * 8 + z

    def ring(k):
        to = lax.rem(zf + k, 16)
        return dev(z_=lax.rem(to, 8), zh_=lax.div(to, 8))

    partners = [sib] + [ring(k) for k in (1, 15, 2, 14)]
    partners += [dev(y_=ymod(k)) for k in range(1, 4)]
    partners += [dev(x_=xmod(k)) for k in range(1, 4)]
    for to in partners:
        pl.semaphore_signal(
            barrier, inc=1, device_id=to, device_id_type=pl.DeviceIdType.MESH
        )
    for load in loads[:2]:
        load.wait()

    def act_rows(r, _):
        rows = pl.ds(pl.multiple_of(r * 16, 16), 16)
        h32 = vin[0, rows, :].astype(F32)
        g32 = vin[1, rows, :].astype(F32)
        u32 = vin[2, rows, :].astype(F32)
        sig = jax.nn.sigmoid(g32)
        hs = h32 * sig
        acts[c, 0, rows, :] = (hs * u32 * (1.0 + g32 * (1.0 - sig))).astype(BF16)
        acts[c, 1, rows, :] = (hs * g32).astype(BF16)
        return 0

    def token_cov(k):
        own_tok = tok[:, pl.ds(pl.multiple_of(j * 128, 128), 128)]
        cols = tok[:, pl.ds(pl.multiple_of(k * 128, 128), 128)]
        covp[0, k] = lax.dot_general(own_tok, cols, TN, preferred_element_type=F32)

    def act_send(r):
        rows = pl.ds(pl.multiple_of(r * 64, 64), 64)
        piece = acts.at[c, :, rows]
        return remote(piece, piece, as_s.at[r], as_r.at[r], sib)

    def act_recv(r):
        rows = pl.ds(pl.multiple_of(r * 64, 64), 64)
        piece = acts.at[oc, :, rows]
        return remote(piece, piece, as_s.at[r], as_r.at[r], sib)

    def local_part(s):
        @pl.when(s < 4)
        def _():
            @pl.when(s == 0)
            def _():
                for load in loads[2:5]:
                    load.wait()

            def rows4(r, _):
                act_rows(s * 4 + r, 0)
                return 0

            lax.fori_loop(0, 4, rows4, 0)
            act_send(s).start()

        @pl.when((s >= 4) & (s < 8))
        def _():
            @pl.when(s == 4)
            def _():
                loads[5].wait()

            token_cov(s * 2 - 8)
            token_cov(s * 2 - 7)

            @pl.when(s == 7)
            def _():
                d0_send(0).start()

    pl.semaphore_wait(barrier, 11)

    def z_up(zz, g):
        return remote(
            half(zz, y, g), half(zz, y, g), zs_s.at[0, g, zz], z_r.at[g, zz], dev(z_=z + 1)
        )

    def z_dn(zz, g):
        return remote(
            half(zz, y, g), half(zz, y, g), zs_s.at[1, g, zz], z_r.at[g, zz], dev(z_=z - 1)
        )

    def y_send(zz, d, g):
        to = dev(y_=ymod(1 if d == 0 else 3))
        return remote(
            half(zz, y, g), half(zz, y, g), ys_s.at[d, g, zz], y_r.at[d, g, zz], to
        )

    def y_recv(zz, d, g):
        src = ymod(3 if d == 0 else 1)
        return remote(
            half(zz, src, g), half(zz, src, g), ys_s.at[d, g, zz], y_r.at[d, g, zz], sib
        )

    def y2_send(zz, d):
        src = ymod(3 if d == 0 else 1)
        to = dev(y_=ymod(1 if d == 0 else 3))
        return remote(half(zz, src, d), half(zz, src, d), y2s_s.at[d, zz], y2_r.at[d, zz], to)

    def y2_recv(zz, d):
        src = ymod(2)
        return remote(half(zz, src, d), half(zz, src, d), y2s_s.at[d, zz], y2_r.at[d, zz], sib)

    def each(s, fn):
        @pl.when((s >= 0) & (z - s >= 0) & (z - s <= 7))
        def _():
            fn(z - s, 0)

        @pl.when((s >= 1) & (z + s <= 7))
        def _():
            fn(z + s, 1)

    def arrive_z(s):
        def fn(zz, d):
            for g in range(2):
                @pl.when(s > 0)
                def _():
                    remote(
                        half(zz, y, g), half(zz, y, g), zs_s.at[0, g, zz], z_r.at[g, zz], sib
                    ).wait_recv()

                if d == 0:
                    @pl.when(z < 7)
                    def _():
                        z_up(zz, g).start()

                    @pl.when((s == 0) & (z > 0))
                    def _():
                        z_dn(zz, g).start()
                else:
                    @pl.when(z > 0)
                    def _():
                        z_dn(zz, g).start()
                y_send(zz, g, g).start()
                y_send(zz, 1 - g, g).start()
        return fn

    def arrive_y(zz, _):
        for d in range(2):
            y_recv(zz, d, d).wait_recv()
            y2_send(zz, d).start()

    def arrive_y2(zz, _):
        for d in range(2):
            y_recv(zz, d, 1 - d).wait_recv()
            y2_recv(zz, d).wait_recv()
        project(zz)

    def x_send(zz):
        to, hh = lax.rem(zz, 4), lax.div(zz, 4)
        return remote(xs.at[zz], xr.at[hh, x], xs_s.at[zz], xs_r.at[hh, x], dev(x_=to))

    def x_recv(k, hh):
        src = xmod(k)
        return remote(xs.at[src], xr.at[hh, src], xs_s.at[src], xs_r.at[hh, src], sib)

    def project(zz):
        t, hh = lax.rem(zz, 4), lax.div(zz, 4)
        wg = w[t, 0, hh].reshape(64, 1792)
        wu = w[t, 1, hh].reshape(64, 1792)
        for cc in range(2):
            part = lax.dot_general(wg, acts[cc, 0], NT, preferred_element_type=F32)
            part += lax.dot_general(wu, acts[cc, 1], NT, preferred_element_type=F32)

            @pl.when(t == x)
            def _():
                pown[hh, cc] = part

            @pl.when(t != x)
            def _():
                xs[zz, cc] = part.astype(BF16)

        @pl.when(t != x)
        def _():
            x_send(zz).start()

    def z8(hh):
        return remote(zsb.at[hh], zrb.at[hh], z8_s.at[hh], z8_r.at[hh], dev(zh_=1 - zh))


    def x_sum(hh):
        for k in range(1, 4):
            x_recv(k, hh).wait_recv()
        for cc in range(2):
            total = pown[hh, cc]
            for k in range(1, 4):
                total = total + xr[hh, xmod(k), cc].astype(F32)
            pown[hh, cc] = total
            zsb[hh, cc] = total.astype(BF16)
        z8(hh).start()

    def hello():
        pl.semaphore_signal(
            hello_sem, inc=1, device_id=ring(2), device_id_type=pl.DeviceIdType.MESH
        )

    def step(s, _):
        @pl.when(s < 4)
        def _():
            hello()

        each(s, arrive_z(s))

        local_part(s)

        each(s - 1, arrive_y)

        @pl.when(s == LAG)
        def _():
            for r in range(4):
                act_recv(r).wait_recv()

        each(s - LAG, arrive_y2)

        def own_sum(hh, _):
            @pl.when(jnp.abs(z - x - 4 * hh) == s - LAG - 1)
            def _():
                x_sum(hh)
            return 0

        lax.fori_loop(0, 2, own_sum, 0)

        @pl.when(s < 4)
        def _():
            pl.semaphore_wait(hello_sem, 1)
        return 0

    def d0_send(m):
        rows = pl.ds(pl.multiple_of(oc * 64, 64), 64)
        return remote(covp.at[m, :, rows], d0r.at[m], d0_s.at[m], d0_r.at[m], sib)

    def d1_send(m, k):
        to = ymod(k)
        return remote(d1s.at[m, to], d1r.at[m, y], d1_s.at[m, to], d1_r.at[m, y], dev(y_=to))

    def d1_recv(m, k):
        src = ymod(k)
        return remote(d1s.at[m, src], d1r.at[m, src], d1_s.at[m, src], d1_r.at[m, src], sib)

    def d2_send(m, k):
        to = zmod(k)
        return remote(d2s.at[m, to], d2r.at[m, z], d2_s.at[m, to], d2_r.at[m, z], dev(z_=to))

    def d2_recv(m, k):
        src = zmod(k)
        return remote(d2s.at[m, src], d2r.at[m, src], d2_s.at[m, src], d2_r.at[m, src], sib)

    def d3_send(m, k):
        to = zmod(k)
        piece = fin.at[m, c, y, z]
        return remote(piece, piece, d3_s.at[m, to], d3_r.at[m, z], dev(z_=to))

    def d3_recv(m, k):
        src = zmod(k)
        piece = fin.at[m, c, y, src]
        return remote(piece, piece, d3_s.at[m, src], d3_r.at[m, src], sib)

    def d4_send(m, k):
        to = ymod(k)
        piece = fin.at[m, c, y]
        return remote(piece, piece, d4_s.at[m, to], d4_r.at[m, y], dev(y_=to))

    def d4_recv(m, k):
        src = ymod(k)
        piece = fin.at[m, c, src]
        return remote(piece, piece, d4_s.at[m, src], d4_r.at[m, src], sib)

    def d5_send(m):
        return remote(fin.at[m, c], fin.at[m, c], d5_s.at[m], d5_r.at[m], sib)

    def d5_recv(m):
        return remote(fin.at[m, oc], fin.at[m, oc], d5_s.at[m], d5_r.at[m], sib)

    def core_sum(m):
        d0_send(m).wait_recv()
        for yy in range(4):
            rows = pl.ds(pl.multiple_of(c * 64 + yy * 16, 16), 16)
            total = covp[m, :, rows, :] + d0r[m, :, yy * 16:(yy + 1) * 16, :]
            covp[m, :, rows, :] = total
            d1s[m, yy] = total.astype(BF16)
        for k in (2, 1, 3):
            d1_send(m, k).start()

    def y_sum(m):
        rows = pl.ds(pl.multiple_of(c * 64 + y * 16, 16), 16)
        total = covp[m, :, rows, :]
        for k in (1, 3, 2):
            d1_recv(m, k).wait_recv()
            total = total + d1r[m, ymod(k)].astype(F32)
        covp[m, :, rows, :] = total
        d2s[m] = total.astype(BF16)
        for k in range(1, 8):
            d2_send(m, k).start()

    def z_sum(m):
        rows = pl.ds(pl.multiple_of(c * 64 + y * 16, 16), 16)
        total = covp[m, z, rows, :]
        for k in range(1, 8):
            d2_recv(m, k).wait_recv()
            total = total + d2r[m, zmod(k)].astype(F32)
        fin[m, c, y, z] = (total * (1.0 / COUNT)).astype(BF16)
        for k in range(1, 8):
            d3_send(m, k).start()

    def z_back(m):
        for k in range(1, 8):
            d3_recv(m, k).wait_recv()
        for k in (2, 1, 3):
            d4_send(m, k).start()

    def y_back(m):
        for k in (1, 3, 2):
            d4_recv(m, k).wait_recv()
        d5_send(m).start()

    def put(m, cc):
        return pltpu.make_async_copy(fin.at[m, cc], fin_out.at[m, cc], out_sem.at[m, cc])

    lax.fori_loop(0, 9 + LAG, step, 0)

    core_sum(0)
    y_sum(0)

    def drain(zz, _):
        for g in range(2):
            @pl.when((z < 7) & (zz <= z))
            def _():
                z_up(zz, g).wait_send()

            @pl.when((z > 0) & (zz >= z))
            def _():
                z_dn(zz, g).wait_send()

            for d in range(2):
                y_send(zz, d, g).wait_send()
            y2_send(zz, g).wait_send()
        return 0

    lax.fori_loop(0, 8, drain, 0)
    for r in range(4):
        act_send(r).wait_send()
    for k in range(1, 4):
        for hh in range(2):
            x_send(xmod(k) + 4 * hh).wait_send()

    def xg_send(k, cc, hh):
        to = xmod(k)
        return remote(
            gs.at[cc, hh], gt.at[hh, x, :, c], xg_s.at[to, cc, hh], xg_r.at[x, c, hh],
            dev(c_=cc, x_=to),
        )

    def xg_recv(k, cc, hh):
        src = xmod(k)
        return remote(
            gs.at[cc, hh], gt.at[hh, src, :, cc], xg_s.at[src, cc, hh], xg_r.at[src, cc, hh], sib
        )

    first = jnp.where(jnp.abs(z - x) <= jnp.abs(z - x - 4), 0, 1)
    for hh in (first, 1 - first):
        z8(hh).wait_recv()
        for cc in range(2):
            grad = (pown[hh, cc] + zrb[hh, cc].astype(F32)).astype(BF16)
            gs[cc, hh] = grad.reshape(4, 16, 256)
        xg_send(0, oc, hh).start()
        for k in (2, 1, 3):
            for cc in range(2):
                xg_send(k, cc, hh).start()
        mine = gs[c, hh]
        for yy in range(4):
            gt[hh, x, yy, c] = mine[yy]
    for hh in range(2):
        xg_recv(0, oc, hh).wait_recv()
    own = gt[zh, x].reshape(128, 256)
    own_out[...] = own

    def cov_cols(k):
        xx = xmod(k)
        for hh in range(2):
            covp[1, hh * 4 + xx] = lax.dot_general(
                own, gt[hh, xx].reshape(128, 256), NT, preferred_element_type=F32
            )

    cov_cols(0)
    z_sum(0)
    for k in (1, 3, 2):
        for cc in range(2):
            for hh in range(2):
                xg_recv(k, cc, hh).wait_recv()
        cov_cols(k)
    d0_send(1).start()
    z_back(0)
    core_sum(1)
    y_back(0)
    y_sum(1)
    put(0, c).start()
    d5_recv(0).wait_recv()
    put(0, oc).start()
    for hh in range(2):
        z8(hh).wait_send()
        xg_send(0, oc, hh).wait_send()
        for k in range(1, 4):
            for cc in range(2):
                xg_send(k, cc, hh).wait_send()

    def drain_sums(m):
        d0_send(m).wait_send()
        for k in range(1, 4):
            d1_send(m, k).wait_send()
        for k in range(1, 8):
            d2_send(m, k).wait_send()

    drain_sums(0)
    z_sum(1)
    for k in range(1, 4):
        d4_send(0, k).wait_send()
    for k in range(1, 8):
        d3_send(0, k).wait_send()
    d5_send(0).wait_send()
    for cc in (c, oc):
        put(0, cc).wait()
    z_back(1)
    drain_sums(1)
    y_back(1)
    put(1, c).start()
    for k in range(1, 8):
        d3_send(1, k).wait_send()
    for k in range(1, 4):
        d4_send(1, k).wait_send()
    d5_recv(1).wait_recv()
    put(1, oc).start()
    d5_send(1).wait_send()
    for cc in (c, oc):
        put(1, cc).wait()


def arrange(fin, own, ig_out, act_out, cov_out):
    ig_out[...] = own[...].astype(F32).T.astype(BF16)
    for m, out in enumerate((act_out, cov_out)):
        for q in range(8):
            for k in range(8):
                out[q * 16:(q + 1) * 16, k * 128:(k + 1) * 128] = fin[m, q // 4, q % 4, k].astype(F32)


def shards(tokens, hidden_grad, gate, up, gate_weight, up_weight):
    sem = pltpu.SemaphoreType.DMA
    fin, own = pl.pallas_call(
        kernel,
        out_shape=(
            jax.ShapeDtypeStruct((2, 2, 4, 8, 16, 128), BF16),
            jax.ShapeDtypeStruct((128, 256), BF16),
        ),
        in_specs=[pl.BlockSpec(memory_space=pltpu.HBM)] * 6,
        out_specs=(
            pl.BlockSpec(memory_space=pl.ANY),
            pl.BlockSpec(memory_space=pltpu.VMEM),
        ),
        scratch_shapes=[
            pltpu.VMEM((256, 1024), BF16),
            pltpu.VMEM((3, 256, 1792), BF16),
            pltpu.VMEM((2, 2, 256, 1792), BF16),
            pltpu.VMEM((4, 2, 2, 4, 16, 1792), BF16),
            pltpu.VMEM((2, 2, 64, 256), F32),
            pltpu.VMEM((8, 2, 64, 256), BF16),
            pltpu.VMEM((2, 4, 2, 64, 256), BF16),
            pltpu.VMEM((2, 2, 64, 256), BF16),
            pltpu.VMEM((2, 2, 64, 256), BF16),
            pltpu.VMEM((2, 2, 4, 16, 256), BF16),
            pltpu.VMEM((2, 4, 4, 2, 16, 256), BF16),
            pltpu.VMEM((2, 8, 128, 128), F32),
            pltpu.VMEM((2, 8, 64, 128), F32),
            pltpu.VMEM((2, 4, 8, 16, 128), BF16),
            pltpu.VMEM((2, 4, 8, 16, 128), BF16),
            pltpu.VMEM((2, 8, 16, 128), BF16),
            pltpu.VMEM((2, 8, 16, 128), BF16),
            pltpu.VMEM((2, 2, 4, 8, 16, 128), BF16),
            sem((6,)), sem((4,)), sem((4,)),
            sem((2, 2, 8)), sem((2, 8)),
            sem((2, 2, 8)), sem((2, 2, 8)),
            sem((2, 8)), sem((2, 8)),
            sem((8,)), sem((2, 4)),
            sem((2,)), sem((2,)),
            sem((4, 2, 2)), sem((4, 2, 2)), sem((2, 2)),
            sem((2,)), sem((2,)),
            sem((2, 4)), sem((2, 4)),
            sem((2, 8)), sem((2, 8)),
            sem((2, 8)), sem((2, 8)),
            sem((2, 4)), sem((2, 4)),
            sem((2,)), sem((2,)),
            pltpu.SemaphoreType.REGULAR,
        ],
        compiler_params=pltpu.CompilerParams(
            collective_id=1, has_side_effects=True, vmem_limit_bytes=60 << 20
        ),
        cost_estimate=pl.CostEstimate(
            flops=2_500_000_000, bytes_accessed=10_000_000, transcendentals=1_000_000
        ),
        name="kfac_stats",
    )(tokens, hidden_grad, gate, up, gate_weight, up_weight)
    return tuple(
        pl.pallas_call(
            arrange,
            out_shape=(
                jax.ShapeDtypeStruct((256, 128), BF16),
                jax.ShapeDtypeStruct((128, 1024), F32),
                jax.ShapeDtypeStruct((128, 1024), F32),
            ),
            in_specs=[pl.BlockSpec(memory_space=pltpu.VMEM)] * 2,
            out_specs=tuple([pl.BlockSpec(memory_space=pltpu.VMEM)] * 3),
            compiler_params=pltpu.CompilerParams(vmem_limit_bytes=16 << 20),
            name="arrange",
        )(fin, own)
    )


def solution(mesh):
    placed = (
        P("dp", None),
        P("dp", "tensor"),
        P("dp", "tensor"),
        P("dp", "tensor"),
        P("dp", "tensor"),
        P("dp", "tensor"),
    )
    return jax.shard_map(
        shards,
        mesh=mesh,
        in_specs=placed,
        out_specs=(P("dp", "tensor"), P("tensor", None), P("tensor", None)),
        check_vma=False,
    )
```

time: 117 us -> 110 us (0.940)
  local copies, waits for them, and re-layouts: 8.42 us -> 1.87 us
    unnamed x15 -> x4, local copies, waits for them, and re-layouts: 8.42 us -> 1.87 us
    pallas_call x1 -> x2, Pallas kernels: 108 us -> 108 us  [the longest x1 107 us: shards(): pl.pallas_call(kernel, out_shape=(jax.ShapeDtypeStruct((2, 2, 4, 8, 16, 1...]
where the time goes in v2:
time: 110 us
  Pallas kernels  108 us (98%)
  local copies, waits for them, and re-layouts  1.87 us (2%)
    pallas_call x1, Pallas kernels, shards(): pl.pallas_call(kernel, out_shape=(jax.ShapeDtypeStruct((2, 2, 4, 8, 16, 1...  107 us

profile of v2, /device:TPU:1, one launch (start us, length us, event | category | flops | bytes accessed | tf_op | source)
XLA Modules:
  0.0 110.2 jit_solution(12206512932489874654)
XLA Ops:
  0.6 106.6 %kfac_stats.1 = (bf16[2,2,4,8,16,128]{5,4,3,2,1,0:T(8,128)(2,1)}, bf16[128,256]{1,0:T(8,128)(2,1)}) custom-call(bf16[256,1024]{1,0:T(8,128)(2,1)} %tok_hbm.1, bf16[256,1792]{1,0:T(8,128)(2,1)} %hid_hbm.1, bf16[256,1792]{1,0:T(8,128)(2,1)} %gate_hbm.1, bf16[256,1792]{1,0:T(8,128)(2,1)} %up_hbm.1, bf16[16,1792]{1,0:T(8,128)(2,1)} %gw_hbm.1, ...), custom_call_target="tpu_custom_call" | custom-call | flops 2500000000 | bytes 10000000 | tf_op jit(solution)/shard_map/kfac_stats/pallas_call | solution.py:519
  107.3 0.0 copy-start
  107.3 1.0 copy-done
  108.3 0.0 copy-start.1
  108.3 0.8 copy-done.1
  109.2 1.0 arrange.1
Async XLA Ops:
  107.3 1.0 copy-start
  108.3 0.8 copy-start.1

commit v3 on v2

--- a/solution.py
+++ b/solution.py
@@ -10,7 +10,7 @@
 NT = (((1,), (1,)), ((), ()))
 TN = (((0,), (0,)), ((), ()))
 COUNT = 16384
-LAG = 3
+LAG, CHAIN, HELLOS = 3, 6, 3
 STOP = 9
 
 
@@ -21,7 +21,7 @@
     covp, d0r, d1s, d1r, d2s, d2r, fin,
     loc_sem, as_s, as_r, zs_s, z_r, ys_s, y_r, y2s_s, y2_r,
     xs_s, xs_r, z8_s, z8_r, xg_s, xg_r, out_sem,
-    d0_s, d0_r, d1_s, d1_r, d2_s, d2_r, d3_s, d3_r, d4_s, d4_r, d5_s, d5_r, hello_sem,
+    d0_s, d0_r, d1_s, d1_r, d2_s, d2_r, d3_s, d3_r, d4_s, d4_r, d5_s, d5_r, hello_sem, far_s,
 ):
     i = lax.axis_index("dp")
     j = lax.axis_index("tensor")
@@ -192,7 +192,7 @@
                     ).wait_recv()
 
                 if d == 0:
-                    @pl.when(z < 7)
+                    @pl.when((z < 7) & (s < CHAIN))
                     def _():
                         z_up(zz, g).start()
 
@@ -200,7 +200,7 @@
                     def _():
                         z_dn(zz, g).start()
                 else:
-                    @pl.when(z > 0)
+                    @pl.when((z > 0) & (s < CHAIN))
                     def _():
                         z_dn(zz, g).start()
                 y_send(zz, g, g).start()
@@ -262,14 +262,35 @@
         z8(hh).start()
 
     def hello():
-        pl.semaphore_signal(
-            hello_sem, inc=1, device_id=ring(2), device_id_type=pl.DeviceIdType.MESH
-        )
+        for d, k in ((0, 2), (1, 14)):
+            pl.semaphore_signal(
+                hello_sem.at[d], inc=1, device_id=ring(k), device_id_type=pl.DeviceIdType.MESH
+            )
+
+    def far(d, k, g):
+        to = dev(z_=z + k if d == 0 else z - k)
+        return remote(half(z, y, g), half(z, y, g), far_s.at[d, g, k], z_r.at[g, z], to)
+
+    def each_far(fn):
+        for k in range(7, CHAIN, -1):
+            @pl.when(z + k <= 7)
+            def _():
+                for g in range(2):
+                    fn(far(0, k, g))
+
+            @pl.when(z - k >= 0)
+            def _():
+                for g in range(2):
+                    fn(far(1, k, g))
 
     def step(s, _):
-        @pl.when(s < 4)
+        @pl.when(s < HELLOS)
         def _():
             hello()
+
+        @pl.when(s == HELLOS)
+        def _():
+            each_far(lambda copy: copy.start())
 
         each(s, arrive_z(s))
 
@@ -292,9 +313,10 @@
 
         lax.fori_loop(0, 2, own_sum, 0)
 
-        @pl.when(s < 4)
-        def _():
-            pl.semaphore_wait(hello_sem, 1)
+        @pl.when(s < HELLOS)
+        def _():
+            for d in range(2):
+                pl.semaphore_wait(hello_sem.at[d], 1)
         return 0
 
     def d0_send(m):
@@ -395,11 +417,11 @@
 
     def drain(zz, _):
         for g in range(2):
-            @pl.when((z < 7) & (zz <= z))
+            @pl.when((z < 7) & (zz <= z) & (z - zz < CHAIN))
             def _():
                 z_up(zz, g).wait_send()
 
-            @pl.when((z > 0) & (zz >= z))
+            @pl.when((z > 0) & (zz >= z) & (zz - z < CHAIN))
             def _():
                 z_dn(zz, g).wait_send()
 
@@ -408,12 +430,6 @@
             y2_send(zz, g).wait_send()
         return 0
 
-    lax.fori_loop(0, 8, drain, 0)
-    for r in range(4):
-        act_send(r).wait_send()
-    for k in range(1, 4):
-        for hh in range(2):
-            x_send(xmod(k) + 4 * hh).wait_send()
 
     def xg_send(k, cc, hh):
         to = xmod(k)
@@ -461,44 +477,49 @@
                 xg_recv(k, cc, hh).wait_recv()
         cov_cols(k)
     d0_send(1).start()
+
+    def drain_sums(m):
+        d0_send(m).wait_send()
+        for k in range(1, 4):
+            d1_send(m, k).wait_send()
+        for k in range(1, 8):
+            d2_send(m, k).wait_send()
+
+    core_sum(1)
+    y_sum(1)
     z_back(0)
-    core_sum(1)
+    lax.fori_loop(0, 8, drain, 0)
+    z_sum(1)
     y_back(0)
-    y_sum(1)
     put(0, c).start()
-    d5_recv(0).wait_recv()
-    put(0, oc).start()
+    each_far(lambda copy: copy.wait_send())
+    for r in range(4):
+        act_send(r).wait_send()
+    for k in range(1, 4):
+        for hh in range(2):
+            x_send(xmod(k) + 4 * hh).wait_send()
     for hh in range(2):
         z8(hh).wait_send()
         xg_send(0, oc, hh).wait_send()
         for k in range(1, 4):
             for cc in range(2):
                 xg_send(k, cc, hh).wait_send()
-
-    def drain_sums(m):
-        d0_send(m).wait_send()
+    drain_sums(0)
+    z_back(1)
+    d5_recv(0).wait_recv()
+    put(0, oc).start()
+    drain_sums(1)
+    for m in range(2):
+        for k in range(1, 8):
+            d3_send(m, k).wait_send()
+    y_back(1)
+    put(1, c).start()
+    for m in range(2):
         for k in range(1, 4):
-            d1_send(m, k).wait_send()
-        for k in range(1, 8):
-            d2_send(m, k).wait_send()
-
-    drain_sums(0)
-    z_sum(1)
-    for k in range(1, 4):
-        d4_send(0, k).wait_send()
-    for k in range(1, 8):
-        d3_send(0, k).wait_send()
+            d4_send(m, k).wait_send()
     d5_send(0).wait_send()
     for cc in (c, oc):
         put(0, cc).wait()
-    z_back(1)
-    drain_sums(1)
-    y_back(1)
-    put(1, c).start()
-    for k in range(1, 8):
-        d3_send(1, k).wait_send()
-    for k in range(1, 4):
-        d4_send(1, k).wait_send()
     d5_recv(1).wait_recv()
     put(1, oc).start()
     d5_send(1).wait_send()
@@ -559,7 +580,8 @@
             sem((2, 8)), sem((2, 8)),
             sem((2, 4)), sem((2, 4)),
             sem((2,)), sem((2,)),
-            pltpu.SemaphoreType.REGULAR,
+            pltpu.SemaphoreType.REGULAR((2,)),
+            sem((2, 2, 8)),
         ],
         compiler_params=pltpu.CompilerParams(
             collective_id=1, has_side_effects=True, vmem_limit_bytes=60 << 20

time: 110 us -> 108 us (0.982)
  Pallas kernels: 108 us -> 105 us
    pallas_call x1, Pallas kernels: 107 us -> 104 us  [shards(): pl.pallas_call(kernel, out_shape=(jax.ShapeDtypeStruct((2, 2, 4, 8, 16, 1...]
where the time goes in v3:
time: 108 us; the launch traced here: 107 us
  Pallas kernels  105 us (97%)
  local copies, waits for them, and re-layouts  1.87 us (2%)
    pallas_call x1, Pallas kernels, shards(): pl.pallas_call(kernel, out_shape=(jax.ShapeDtypeStruct((2, 2, 4, 8, 16, 1...  104 us

profile of v3, /device:TPU:1, one launch (start us, length us, event | category | flops | bytes accessed | tf_op | source)
XLA Modules:
  0.0 107.5 jit_solution(11761987436131169529)
XLA Ops:
  0.6 104.0 %kfac_stats.1 = (bf16[2,2,4,8,16,128]{5,4,3,2,1,0:T(8,128)(2,1)}, bf16[128,256]{1,0:T(8,128)(2,1)}) custom-call(bf16[256,1024]{1,0:T(8,128)(2,1)} %tok_hbm.1, bf16[256,1792]{1,0:T(8,128)(2,1)} %hid_hbm.1, bf16[256,1792]{1,0:T(8,128)(2,1)} %gate_hbm.1, bf16[256,1792]{1,0:T(8,128)(2,1)} %up_hbm.1, bf16[16,1792]{1,0:T(8,128)(2,1)} %gw_hbm.1, ...), custom_call_target="tpu_custom_call" | custom-call | flops 2500000000 | bytes 10000000 | tf_op jit(solution)/shard_map/kfac_stats/pallas_call | solution.py:540
  104.6 0.0 copy-start
  104.6 1.0 copy-done
  105.6 0.0 copy-start.1
  105.6 0.8 copy-done.1
  106.5 1.0 arrange.1
Async XLA Ops:
  104.6 1.0 copy-start
  105.6 0.8 copy-start.1

commit v4 on v3

--- a/solution.py
+++ b/solution.py
@@ -296,7 +296,6 @@
 
         local_part(s)
 
-        each(s - 1, arrive_y)
 
         @pl.when(s == LAG)
         def _():
@@ -304,6 +303,7 @@
                 act_recv(r).wait_recv()
 
         each(s - LAG, arrive_y2)
+        each(s - 1, arrive_y)
 
         def own_sum(hh, _):
             @pl.when(jnp.abs(z - x - 4 * hh) == s - LAG - 1)

time: 108 us -> 107 us (level)
  no operation moved by 1% of the time
where the time goes in v4:
time: 107 us
  Pallas kernels  104 us (97%)
  local copies, waits for them, and re-layouts  1.87 us (2%)
    pallas_call x1, Pallas kernels, shards(): pl.pallas_call(kernel, out_shape=(jax.ShapeDtypeStruct((2, 2, 4, 8, 16, 1...  103 us

profile of v4, /device:TPU:1, one launch (start us, length us, event | category | flops | bytes accessed | tf_op | source)
XLA Modules:
  0.0 106.6 jit_solution(8834244895357389770)
XLA Ops:
  0.6 103.0 %kfac_stats.1 = (bf16[2,2,4,8,16,128]{5,4,3,2,1,0:T(8,128)(2,1)}, bf16[128,256]{1,0:T(8,128)(2,1)}) custom-call(bf16[256,1024]{1,0:T(8,128)(2,1)} %tok_hbm.1, bf16[256,1792]{1,0:T(8,128)(2,1)} %hid_hbm.1, bf16[256,1792]{1,0:T(8,128)(2,1)} %gate_hbm.1, bf16[256,1792]{1,0:T(8,128)(2,1)} %up_hbm.1, bf16[16,1792]{1,0:T(8,128)(2,1)} %gw_hbm.1, ...), custom_call_target="tpu_custom_call" | custom-call | flops 2500000000 | bytes 10000000 | tf_op jit(solution)/shard_map/kfac_stats/pallas_call | solution.py:540
  103.7 0.0 copy-start
  103.7 1.0 copy-done
  104.7 0.0 copy-start.1
  104.7 0.8 copy-done.1
  105.6 1.0 arrange.1
Async XLA Ops:
  103.7 1.0 copy-start
  104.7 0.8 copy-start.1

commit v5 on v4

--- a/solution.py
+++ b/solution.py
@@ -100,7 +100,9 @@
     def token_cov(k):
         own_tok = tok[:, pl.ds(pl.multiple_of(j * 128, 128), 128)]
         cols = tok[:, pl.ds(pl.multiple_of(k * 128, 128), 128)]
-        covp[0, k] = lax.dot_general(own_tok, cols, TN, preferred_element_type=F32)
+        covp[0, lax.div(k, 4), lax.rem(k, 4)] = lax.dot_general(
+            own_tok, cols, TN, preferred_element_type=F32
+        )
 
     def act_send(r):
         rows = pl.ds(pl.multiple_of(r * 64, 64), 64)
@@ -138,7 +140,8 @@
 
             @pl.when(s == 7)
             def _():
-                d0_send(0).start()
+                for k in range(4):
+                    d0_send(0, k).start()
 
     pl.semaphore_wait(barrier, 11)
 
@@ -319,9 +322,12 @@
                 pl.semaphore_wait(hello_sem.at[d], 1)
         return 0
 
-    def d0_send(m):
+    def d0_send(m, k):
+        xx = xmod(k)
         rows = pl.ds(pl.multiple_of(oc * 64, 64), 64)
-        return remote(covp.at[m, :, rows], d0r.at[m], d0_s.at[m], d0_r.at[m], sib)
+        return remote(
+            covp.at[m, :, xx, rows], d0r.at[m, :, xx], d0_s.at[m, xx], d0_r.at[m, xx], sib
+        )
 
     def d1_send(m, k):
         to = ymod(k)
@@ -366,29 +372,30 @@
         return remote(fin.at[m, oc], fin.at[m, oc], d5_s.at[m], d5_r.at[m], sib)
 
     def core_sum(m):
-        d0_send(m).wait_recv()
+        for k in range(4):
+            d0_send(m, k).wait_recv()
         for yy in range(4):
             rows = pl.ds(pl.multiple_of(c * 64 + yy * 16, 16), 16)
-            total = covp[m, :, rows, :] + d0r[m, :, yy * 16:(yy + 1) * 16, :]
-            covp[m, :, rows, :] = total
-            d1s[m, yy] = total.astype(BF16)
+            total = covp[m, :, :, rows, :] + d0r[m, :, :, yy * 16:(yy + 1) * 16, :]
+            covp[m, :, :, rows, :] = total
+            d1s[m, yy] = total.reshape(8, 16, 128).astype(BF16)
         for k in (2, 1, 3):
             d1_send(m, k).start()
 
     def y_sum(m):
         rows = pl.ds(pl.multiple_of(c * 64 + y * 16, 16), 16)
-        total = covp[m, :, rows, :]
+        total = covp[m, :, :, rows, :].reshape(8, 16, 128)
         for k in (1, 3, 2):
             d1_recv(m, k).wait_recv()
             total = total + d1r[m, ymod(k)].astype(F32)
-        covp[m, :, rows, :] = total
+        covp[m, :, :, rows, :] = total.reshape(2, 4, 16, 128)
         d2s[m] = total.astype(BF16)
         for k in range(1, 8):
             d2_send(m, k).start()
 
     def z_sum(m):
         rows = pl.ds(pl.multiple_of(c * 64 + y * 16, 16), 16)
-        total = covp[m, z, rows, :]
+        total = covp[m, lax.div(z, 4), lax.rem(z, 4), rows, :]
         for k in range(1, 8):
             d2_recv(m, k).wait_recv()
             total = total + d2r[m, zmod(k)].astype(F32)
@@ -465,21 +472,23 @@
     def cov_cols(k):
         xx = xmod(k)
         for hh in range(2):
-            covp[1, hh * 4 + xx] = lax.dot_general(
+            covp[1, hh, xx] = lax.dot_general(
                 own, gt[hh, xx].reshape(128, 256), NT, preferred_element_type=F32
             )
 
     cov_cols(0)
+    d0_send(1, 0).start()
     z_sum(0)
     for k in (1, 3, 2):
         for cc in range(2):
             for hh in range(2):
                 xg_recv(k, cc, hh).wait_recv()
         cov_cols(k)
-    d0_send(1).start()
+        d0_send(1, k).start()
 
     def drain_sums(m):
-        d0_send(m).wait_send()
+        for k in range(4):
+            d0_send(m, k).wait_send()
         for k in range(1, 4):
             d1_send(m, k).wait_send()
         for k in range(1, 8):
@@ -560,8 +569,8 @@
             pltpu.VMEM((2, 2, 64, 256), BF16),
             pltpu.VMEM((2, 2, 4, 16, 256), BF16),
             pltpu.VMEM((2, 4, 4, 2, 16, 256), BF16),
-            pltpu.VMEM((2, 8, 128, 128), F32),
-            pltpu.VMEM((2, 8, 64, 128), F32),
+            pltpu.VMEM((2, 2, 4, 128, 128), F32),
+            pltpu.VMEM((2, 2, 4, 64, 128), F32),
             pltpu.VMEM((2, 4, 8, 16, 128), BF16),
             pltpu.VMEM((2, 4, 8, 16, 128), BF16),
             pltpu.VMEM((2, 8, 16, 128), BF16),
@@ -574,7 +583,7 @@
             sem((8,)), sem((2, 4)),
             sem((2,)), sem((2,)),
             sem((4, 2, 2)), sem((4, 2, 2)), sem((2, 2)),
-            sem((2,)), sem((2,)),
+            sem((2, 4)), sem((2, 4)),
             sem((2, 4)), sem((2, 4)),
             sem((2, 8)), sem((2, 8)),
             sem((2, 8)), sem((2, 8)),

time: 107 us -> 107 us (level)
  no operation moved by 1% of the time
where the time goes in v5:
time: 107 us; the launch traced here: 106 us
  Pallas kernels  104 us (97%)
  local copies, waits for them, and re-layouts  1.87 us (2%)
    pallas_call x1, Pallas kernels, shards(): pl.pallas_call(kernel, out_shape=(jax.ShapeDtypeStruct((2, 2, 4, 8, 16, 1...  103 us

profile of v5, /device:TPU:1, one launch (start us, length us, event | category | flops | bytes accessed | tf_op | source)
XLA Modules:
  0.0 106.4 jit_solution(17021741172218851058)
XLA Ops:
  0.6 102.9 %kfac_stats.1 = (bf16[2,2,4,8,16,128]{5,4,3,2,1,0:T(8,128)(2,1)}, bf16[128,256]{1,0:T(8,128)(2,1)}) custom-call(bf16[256,1024]{1,0:T(8,128)(2,1)} %tok_hbm.1, bf16[256,1792]{1,0:T(8,128)(2,1)} %hid_hbm.1, bf16[256,1792]{1,0:T(8,128)(2,1)} %gate_hbm.1, bf16[256,1792]{1,0:T(8,128)(2,1)} %up_hbm.1, bf16[16,1792]{1,0:T(8,128)(2,1)} %gw_hbm.1, ...), custom_call_target="tpu_custom_call" | custom-call | flops 2500000000 | bytes 10000000 | tf_op jit(solution)/shard_map/kfac_stats/pallas_call | solution.py:549
  103.5 0.0 copy-start
  103.5 1.0 copy-done
  104.6 0.0 copy-start.1
  104.6 0.8 copy-done.1
  105.4 1.0 arrange.1
Async XLA Ops:
  103.5 1.0 copy-start
  104.6 0.8 copy-start.1
